TPU v7x, 32 devices: a whole 2x2x4 slice. The times are simulated.
32 devices in a mesh: req: 4 (over y, x), exp: 8 (over z, core).
Axes of the slice: x: 2, y: 2, z: 4, core: 2. Of those that a mesh axis runs over, the one named last changes fastest.
Arguments:
- hidden_in: bfloat16 [4096, 1536], P(('req', 'exp')), may hold values from -6 to 6
- attn_gain: bfloat16 [1536], replicated, may hold values from 0.099609375 to 1.8984375
- w_query: bfloat16 [1536, 1536], replicated, may hold values from -0.625 to 0.625
- w_key: bfloat16 [1536, 512], replicated, may hold values from -0.625 to 0.625
- w_value: bfloat16 [1536, 512], replicated, may hold values from -0.15625 to 0.15625
- w_out: bfloat16 [1536, 1536], replicated, may hold values from -0.15625 to 0.15625
- cache_kv: bfloat16 [4, 384, 1024], P('req', 'exp'), may hold values from -128 to 128
- cache_len: int32 [4], P('req'), may hold values from 12 to 384, as said below
- moe_gain: bfloat16 [1536], replicated, may hold values from 0.099609375 to 1.8984375
- expert_ids: int32 [4096, 8], P(('req', 'exp')), may hold values from 0 to 39, all different within a row; in each aligned block of 128 rows (0 to 127, 128 to 255, ...) at most 26 rows name the same one
- expert_weights: bfloat16 [4096, 8], P(('req', 'exp')), may hold values from 0.019897461 to 0.5
- w_gate_up: bfloat16 [8, 20, 1536, 256], P('exp', None, 'req'), may hold values from -0.15625 to 0.15625
- w_down: bfloat16 [8, 20, 128, 1536], P('exp', None, None, 'req'), may hold values from -0.25 to 0.25
Outputs:
- attended: bfloat16 [4096, 1536], P(('req', 'exp'))
- layer_out: bfloat16 [4096, 1536], P(('req', 'exp'))
Inputs may be any that keep to these rules, and one draw needn't show every extreme that they name: `cache_len`: cached positions of each request; some request has exactly 384, some exactly 12. `expert_ids`: each row names 8 different experts. Among the rows of one device no expert is named more than 26 times; in some devices' rows one expert is named exactly 26 times.
All inputs are finite; a program needn't handle non-finite values.
Results may differ from a plain program's by a relative error of at most 0.009.
Values may be sent and summed in bfloat16 or wider, within the bound.
A program may use at most 256 MiB of HBM per device.

v0:
```python
import jax
import jax.numpy as jnp
from jax import lax
from jax.sharding import PartitionSpec as P

HEAD_DIM = 64
EXPERTS = 40
TOPK = 8
PIECES = 4
MOST = 26


rope_base = 10000.0
attn_scale = 0.015625
residual_scale = 1.0
norm_eps = 1e-06
neg_fill = -1e30
key_block = 512


def rms_scale(values, gain):
    widened = values.astype(jnp.float32)
    mean_sq = jnp.mean(widened * widened, axis=-1, keepdims=True)
    return (widened * lax.rsqrt(mean_sq + norm_eps) * gain.astype(jnp.float32)).astype(jnp.bfloat16)


def rotate(projected, positions, head_count, head_dim):
    row_count = projected.shape[0]
    shaped = projected.reshape(row_count, head_count, head_dim)
    half_dim = head_dim // 2
    inverse_freq = rope_base ** (-(jnp.arange(half_dim, dtype=jnp.float32) * 2.0 / head_dim))
    angles = positions.astype(jnp.float32)[:, None] * inverse_freq[None, :]
    cosine = jnp.cos(angles)[:, None, :]
    sinus = jnp.sin(angles)[:, None, :]
    lower_half = shaped[..., :half_dim]
    upper_half = shaped[..., half_dim:]
    turned = jnp.concatenate(
        [lower_half * cosine - upper_half * sinus, upper_half * cosine + lower_half * sinus],
        axis=-1,
    )
    return turned.reshape(row_count, head_count * head_dim).astype(jnp.bfloat16)


def attend_block(running, queries, block_rows, visible, kv_width):
    run_max, run_sum, run_acc = running
    kv_heads = run_max.shape[0]
    head_dim = run_acc.shape[-1]
    block_size = block_rows.shape[0]
    key_heads = block_rows[:, :kv_width].reshape(block_size, kv_heads, head_dim)
    value_heads = block_rows[:, kv_width:].reshape(block_size, kv_heads, head_dim)
    scores = (
        jnp.einsum("tkgd,rkd->kgtr", queries, key_heads, preferred_element_type=jnp.float32)
        * attn_scale
    )
    scores = jnp.where(visible[None, None], scores, neg_fill)
    new_max = jnp.maximum(run_max, jnp.max(scores, axis=-1))
    weights = jnp.where(visible[None, None], jnp.exp(scores - new_max[..., None]), 0.0)
    factor = jnp.exp(run_max - new_max)
    new_sum = run_sum * factor + jnp.sum(weights, axis=-1)
    new_acc = run_acc * factor[..., None] + jnp.einsum(
        "kgtr,rkd->kgtd",
        weights.astype(jnp.bfloat16),
        value_heads,
        preferred_element_type=jnp.float32,
    )
    return (new_max, new_sum, new_acc)


def shards(
    hidden_in,
    attn_gain,
    w_query,
    w_key,
    w_value,
    w_out,
    cache_kv,
    cache_len,
    moe_gain,
    expert_ids,
    expert_weights,
    w_gate_up,
    w_down,
):
    rows_here = hidden_in.shape[0]
    width = hidden_in.shape[1]
    kv_width = w_key.shape[1]
    kv_heads = kv_width // HEAD_DIM
    head_count = w_query.shape[1] // HEAD_DIM
    group_size = head_count // kv_heads
    position_exp = lax.axis_index("exp")
    length = cache_len[0]
    cache_rows = cache_kv[0]
    cache_count = cache_rows.shape[0]
    gate_up_full, down_full = (
        lax.all_gather(w_gate_up[0], "req", axis=1, tiled=True),
        lax.all_gather(w_down[0], "req", axis=2, tiled=True),
    )
    normed = rms_scale(hidden_in, attn_gain)
    query_pos = position_exp * rows_here + jnp.arange(rows_here, dtype=jnp.int32)
    positions = length + query_pos
    query = rotate(
        jnp.dot(normed, w_query, preferred_element_type=jnp.float32),
        positions,
        head_count,
        HEAD_DIM,
    )
    keys_new = rotate(
        jnp.dot(normed, w_key, preferred_element_type=jnp.float32), positions, kv_heads, HEAD_DIM
    )
    values_new = jnp.dot(normed, w_value, preferred_element_type=jnp.float32).astype(jnp.bfloat16)
    new_kv = jnp.concatenate([keys_new, values_new], axis=1)
    queries = query.reshape(rows_here, kv_heads, group_size, HEAD_DIM)
    initial = (
        jnp.full((kv_heads, group_size, rows_here), neg_fill, jnp.float32),
        jnp.zeros((kv_heads, group_size, rows_here), jnp.float32),
        jnp.zeros((kv_heads, group_size, rows_here, HEAD_DIM), jnp.float32),
    )
    shard_rows = cache_count + rows_here
    joined = jnp.concatenate([cache_rows, new_kv], axis=0)
    running = initial
    piece = lax.all_gather(joined, "exp", axis=0, tiled=True)
    first_row = jnp.int32(0)
    key_count = piece.shape[0]
    for offset in range(0, key_count, key_block):
        block_size = min(key_block, key_count - offset)
        key_index = first_row + offset + jnp.arange(block_size, dtype=jnp.int32)
        owner = key_index // shard_rows
        within = key_index - owner * shard_rows
        cached = within < cache_count
        cache_pos = owner * cache_count + within
        new_pos = owner * rows_here + within - cache_count
        running = attend_block(
            running,
            queries,
            piece[offset : offset + block_size],
            jnp.where(
                cached[None, :],
                (cache_pos < length)[None, :],
                new_pos[None, :] <= query_pos[:, None],
            ),
            kv_width,
        )
    run_max, run_sum, run_acc = running
    context = (
        (run_acc / run_sum[..., None])
        .transpose(2, 0, 1, 3)
        .reshape(rows_here, head_count * HEAD_DIM)
        .astype(jnp.bfloat16)
    )
    projected = jnp.dot(context, w_out, preferred_element_type=jnp.float32)
    attended = (hidden_in.astype(jnp.float32) + residual_scale * projected).astype(jnp.bfloat16)
    moe_in = rms_scale(attended, moe_gain)
    block_experts = gate_up_full.shape[0]
    slice_width = down_full.shape[1]
    flat_ids = expert_ids.reshape(-1)
    matches = (flat_ids[:, None] == jnp.arange(EXPERTS, dtype=jnp.int32)[None, :]).astype(jnp.int32)
    slot_rank = jnp.sum((jnp.cumsum(matches, axis=0) - matches) * matches, axis=1)
    slot_index = flat_ids * MOST + slot_rank
    token_of = jnp.arange(flat_ids.shape[0], dtype=jnp.int32) // TOPK
    sectioned = (
        jnp.zeros((EXPERTS * MOST, width), jnp.bfloat16).at[slot_index].set(moe_in[token_of])
    )
    blocks = EXPERTS // block_experts
    outgoing = jnp.broadcast_to(
        sectioned.reshape(blocks, 1, block_experts, MOST, width),
        (blocks, PIECES, block_experts, MOST, width),
    )
    outgoing = outgoing.reshape(blocks * PIECES, block_experts, MOST, width)
    gate_up = jnp.einsum(
        "sgmd,gdf->sgmf",
        lax.all_to_all(outgoing, "exp", split_axis=0, concat_axis=0, tiled=True),
        gate_up_full,
        preferred_element_type=jnp.float32,
    )
    activated = (jax.nn.silu(gate_up[..., :slice_width]) * gate_up[..., slice_width:]).astype(
        jnp.bfloat16
    )
    computed = jnp.einsum(
        "sgmf,gfd->sgmd", activated, down_full, preferred_element_type=jnp.float32
    ).astype(jnp.bfloat16)
    returned = lax.all_to_all(computed, "exp", split_axis=0, concat_axis=0, tiled=True)
    summed = jnp.sum(
        returned.reshape(blocks, PIECES, block_experts, MOST, width), axis=1, dtype=jnp.float32
    )
    summed = summed.reshape(EXPERTS * MOST, width)
    picked = summed[slot_index] * expert_weights.reshape(-1).astype(jnp.float32)[:, None]
    mixture = jnp.sum(picked.reshape(rows_here, TOPK, width), axis=1)
    layer_out = (attended.astype(jnp.float32) + residual_scale * mixture).astype(jnp.bfloat16)
    return (attended, layer_out)


def solution(mesh):
    in_specs = (
        P(("req", "exp"), None),
        P(),
        P(),
        P(),
        P(),
        P(),
        P("req", "exp", None),
        P("req"),
        P(),
        P(("req", "exp"), None),
        P(("req", "exp"), None),
        P("exp", None, "req", None),
        P("exp", None, None, "req"),
    )
    out_specs = (P(("req", "exp"), None), P(("req", "exp"), None))
    return jax.shard_map(shards, mesh=mesh, in_specs=in_specs, out_specs=out_specs, check_vma=False)
```

profile of v0, /device:TPU:0, one launch (start us, length us, event | category | flops | bytes accessed | tf_op | source)
XLA Modules:
  0.0 878.0 jit_solution(16098542286415799547)
XLA Ops:
  12.0 2.0 convolution_convert_fusion
  15.9 11.3 %reduce-window.6 = s32[40,8,128]{2,1,0:T(8,128)S(1)} reduce-window(s32[40,8,128]{2,1,0:T(8,128)S(1)} %fusion.75, s32[]{:T(128)} %constant.37.clone.1), window={size=1x1x128 pad=0_0x0_0x127_0}, to_apply=%region_7.8 | reduce-window | flops 5201920 | bytes 327684 | tf_op jit(solution)/shard_map/reduce-window
  27.9 4.3 fusion.101
  33.9 20.0 %all-gather.6.cloned.1.call-done = bf16[1408,1024]{1,0:T(8,128)(2,1)} async-done(((bf16[176,1024]{1,0:T(8,128)(2,1)}), bf16[1408,1024]{1,0:T(8,128)(2,1)}) %all-gather.6.cloned.1.call-update) | async-done | bytes 2883600 | tf_op jit(solution)/shard_map/all_gather | solution.py:121
  53.9 2.5 fusion.110
  59.8 1.9 copy.54
  63.1 2.0 fusion.11
  77.7 18.1 %scatter_custom_fusion = bf16[1040,1536]{1,0:T(8,128)(2,1)} fusion(s32[1024]{0:T(1024)S(1)} %bitcast.238, bf16[128,1536]{1,0:T(8,128)(2,1)S(1)} %fusion.70, s32[1024]{0:T(1024)S(1)} %broadcast_clamp_fusion.1, bf16[]{:T(256)} %constant.90.clone.1), kind=kCustom, calls=%fused_computation.26 | custom fusion | bytes 3194882 | tf_op jit(solution)/shard_map/scatter | solution.py:161
  95.8 5.7 broadcast_in_dim.166
  101.4 3.9 copy.62
  105.3 5.5 broadcast_in_dim.167
  110.9 5.6 all-to-all-start
  117.2 86.2 %all-gather.8.cloned.1.call-done = bf16[1,20,1536,256]{3,2,1,0:T(8,128)(2,1)} async-done(((bf16[1,20,384,256]{3,2,1,0:T(8,128)(2,1)}), bf16[1,20,1536,256]{3,2,1,0:T(8,128)(2,1)}) %all-gather.8.cloned.1.call-update) | async-done | bytes 15728656 | tf_op jit(solution)/shard_map/all_gather | solution.py:95
  203.4 245.8 %all-to-all-done = bf16[8,20,26,1536]{3,1,2,0:T(8,128)(2,1)} async-done(((bf16[8,20,26,1536]{3,1,2,0:T(8,128)(2,1)}), bf16[8,20,26,1536]{3,1,2,0:T(8,128)(2,1)}, u32[]{:S(2)}, u32[]{:S(2)}) %all-to-all-start) | async-done | bytes 12779552 | tf_op jit(solution)/shard_map/all_to_all | solution.py:171
  449.2 16.8 %fusion.23 = f32[8,20,26,256]{3,2,0,1:T(8,128)} fusion(bf16[1,20,1536,256]{3,2,1,0:T(8,128)(2,1)} %all-gather.8.cloned.1.call-done, bf16[8,20,26,1536]{3,1,2,0:T(8,128)(2,1)} %all-to-all-done), kind=kOutput, calls=%fused_computation.35 | convolution fusion | flops 3271557120 | bytes 32768000 | tf_op jit(solution)/shard_map/sgmd,gdf->sgmf/dot_general | solution.py:169
  466.1 11.8 %convert_bitcast_fusion = bf16[8,20,26,1536]{3,2,0,1:T(8,128)(2,1)} fusion(bf16[1,20,128,1536]{3,2,1,0:T(8,128)(2,1)} %all-gather.10.cloned.1.call-done, f32[8,20,26,256]{3,2,0,1:T(8,128)} %fusion.23), kind=kOutput, calls=%fused_computation.7 | convolution fusion | flops 1645363200 | bytes 24903680 | tf_op jit(solution)/shard_map/sgmf,gfd->sgmd/dot_general | solution.py:178
  477.9 14.0 %copy.64 = bf16[8,20,26,1536]{3,1,2,0:T(8,128)(2,1)} copy(bf16[8,20,26,1536]{3,2,0,1:T(8,128)(2,1)} %convert_bitcast_fusion) | data formatting | bytes 25559040 | tf_op jit(solution)/shard_map/convert_element_type | solution.py:180
  491.9 6.0 all-to-all-start.1
  498.0 332.6 %all-to-all-done.1 = bf16[8,20,26,1536]{3,1,2,0:T(8,128)(2,1)} async-done(((bf16[8,20,26,1536]{3,1,2,0:T(8,128)(2,1)}), bf16[8,20,26,1536]{3,1,2,0:T(8,128)(2,1)}, u32[]{:S(2)}, u32[]{:S(2)}) %all-to-all-start.1) | async-done | bytes 12779552 | tf_op jit(solution)/shard_map/all_to_all | solution.py:181
  830.7 9.3 %convert_reduce_fusion = f32[2,20,26,1536]{3,1,2,0:T(8,128)S(1)} fusion(bf16[8,20,26,1536]{3,1,2,0:T(8,128)(2,1)} %all-to-all-done.1), kind=kLoop, calls=%fused_computation.3 | loop fusion | flops 11182080 | bytes 19169280 | tf_op jit(solution)/shard_map/reduce_sum | solution.py:182
  840.0 6.8 copy.66
  846.8 7.8 reshape.533
  854.6 10.7 %gather_fusion = f32[1024,1536]{1,0:T(8,128)} fusion(f32[1040,1536]{1,0:T(8,128)} %reshape.533, s32[1024]{0:T(1024)S(1)} %broadcast_clamp_fusion), kind=kCustom, calls=%fused_computation.1 | custom fusion | bytes 12587008 | tf_op jit(solution)/shard_map/gather | solution.py:186
  865.3 5.1 fusion.4
  (90 shorter events, 27.0 us)
Async XLA Ops:
  7.2 2.9 copy-start
  7.2 6.8 copy-start.5
  7.2 46.7 %all-gather.6.cloned.1.call-start = ((), (), s32[]{:S(2)}) async-start(), calls=%async_computation.2 | async-start | bytes 3244032 | tf_op jit(solution)/shard_map/all_gather | solution.py:121
  9.9 5.7 copy-start.6
  10.1 5.8 copy-start.7
  11.8 16.0 %copy-start.2 = (bf16[128,1536]{1,0:T(8,128)(2,1)S(1)}, bf16[128,1536]{1,0:T(8,128)(2,1)}, u32[]{:S(2)}) copy-start(bf16[128,1536]{1,0:T(8,128)(2,1)} %param.13) | copy-start | bytes 1179652
  14.8 188.6 %all-gather.8.cloned.1.call-start = ((), (), s32[]{:S(2)}) async-start(), calls=%async_computation.3 | async-start | bytes 19660800 | tf_op jit(solution)/shard_map/all_gather | solution.py:95
  68.4 3.0 copy-start.4
  71.5 5.0 slice-start
  73.2 3.3 slice-start.1
  77.5 792.9 %copy-start.3 = (bf16[128,1536]{1,0:T(8,128)(2,1)}, bf16[128,1536]{1,0:T(8,128)(2,1)S(1)}, u32[]{:S(2)}) copy-start(bf16[128,1536]{1,0:T(8,128)(2,1)S(1)} %get-tuple-element.30) | copy-start | bytes 1179652
  110.9 338.4 %all-to-all-start = ((bf16[8,20,26,1536]{3,1,2,0:T(8,128)(2,1)}), bf16[8,20,26,1536]{3,1,2,0:T(8,128)(2,1)}, u32[]{:S(2)}, u32[]{:S(2)}) async-start(bf16[8,20,26,1536]{3,1,2,0:T(8,128)(2,1)} %bitcast.219), calls=%async_computation | async-start | bytes 30670848 | tf_op jit(solution)/shard_map/all_to_all | solution.py:171
  116.5 349.6 %all-gather.10.cloned.1.call-start = ((), (), s32[]{:S(2)}) async-start(), calls=%async_computation.4 | async-start | bytes 9830400 | tf_op jit(solution)/shard_map/all_gather | solution.py:96
  491.9 6.0 copy-start.8
  491.9 338.7 %all-to-all-start.1 = ((bf16[8,20,26,1536]{3,1,2,0:T(8,128)(2,1)}), bf16[8,20,26,1536]{3,1,2,0:T(8,128)(2,1)}, u32[]{:S(2)}, u32[]{:S(2)}) async-start(bf16[8,20,26,1536]{3,1,2,0:T(8,128)(2,1)} %copy.64), calls=%async_computation.1 | async-start | bytes 30670848 | tf_op jit(solution)/shard_map/all_to_all | solution.py:181
  854.6 16.6 %copy-start.1 = (bf16[1536,512]{1,0:T(8,128)(2,1)S(1)}, bf16[1536,512]{1,0:T(8,128)(2,1)}, u32[]{:S(2)}) copy-start(bf16[1536,512]{1,0:T(8,128)(2,1)} %param.16) | copy-start | bytes 4718596
Sparse Core Ops, SparseCore 0:
  15.0 38.9 all-gather.5
  55.7 147.6 all-gather.7
  205.2 83.0 all-gather.9
where the time goes:
time: 883 us; the launch traced here: 878 us
  waiting for transfers between devices  686 us (78%)
  local copies, waits for them, and re-layouts  82.8 us (9%)
  matrix products  46.8 us (5%)
  other arithmetic  35.4 us (4%)
  between operations  15.2 us (2%)
  starting transfers between devices  11.7 us (1%)
    all_to_all x1, waiting for transfers between devices, shards(): lax.all_to_all(computed, 'exp', split_axis=0, concat_axis=0, tiled=True)  333 us
    all_to_all x1, waiting for transfers between devices, shards(): lax.all_to_all(outgoing, 'exp', split_axis=0, concat_axis=0, tiled=True)  246 us
    all_gather x1, waiting for transfers between devices, shards(): lax.all_gather(w_gate_up[0], 'req', axis=1, tiled=True)  86.2 us
    all_gather x1, waiting for transfers between devices, shards(): piece = lax.all_gather(joined, 'exp', axis=0, tiled=True)  20 us
    scatter x1, local copies, waits for them, and re-layouts, shards(): jnp.zeros((EXPERTS * MOST, width), jnp.bfloat16).at[slot_index]  18.1 us
  transfers between devices with their start and end apart: 5, of which 4 were waited for; matrix products, arithmetic and copies ran while one was open for 10% of the time, Pallas kernels for 0%

commit v1 on v0

--- a/solution.py
+++ b/solution.py
@@ -1,13 +1,13 @@
 import jax
 import jax.numpy as jnp
 from jax import lax
+from jax.experimental import pallas as pl
+from jax.experimental.pallas import tpu as pltpu
 from jax.sharding import PartitionSpec as P
 
 HEAD_DIM = 64
-EXPERTS = 40
-TOPK = 8
 PIECES = 4
-MOST = 26
+ROUTE_LANES = 128
 
 
 rope_base = 10000.0
@@ -92,8 +92,8 @@
     cache_rows = cache_kv[0]
     cache_count = cache_rows.shape[0]
     gate_up_full, down_full = (
-        lax.all_gather(w_gate_up[0], "req", axis=1, tiled=True),
-        lax.all_gather(w_down[0], "req", axis=2, tiled=True),
+        lax.all_gather(w_gate_up[0], "req", axis=0),
+        lax.all_gather(w_down[0], "req", axis=0),
     )
     normed = rms_scale(hidden_in, attn_gain)
     query_pos = position_exp * rows_here + jnp.arange(rows_here, dtype=jnp.int32)
@@ -150,43 +150,91 @@
     projected = jnp.dot(context, w_out, preferred_element_type=jnp.float32)
     attended = (hidden_in.astype(jnp.float32) + residual_scale * projected).astype(jnp.bfloat16)
     moe_in = rms_scale(attended, moe_gain)
-    block_experts = gate_up_full.shape[0]
-    slice_width = down_full.shape[1]
-    flat_ids = expert_ids.reshape(-1)
-    matches = (flat_ids[:, None] == jnp.arange(EXPERTS, dtype=jnp.int32)[None, :]).astype(jnp.int32)
-    slot_rank = jnp.sum((jnp.cumsum(matches, axis=0) - matches) * matches, axis=1)
-    slot_index = flat_ids * MOST + slot_rank
-    token_of = jnp.arange(flat_ids.shape[0], dtype=jnp.int32) // TOPK
-    sectioned = (
-        jnp.zeros((EXPERTS * MOST, width), jnp.bfloat16).at[slot_index].set(moe_in[token_of])
-    )
-    blocks = EXPERTS // block_experts
-    outgoing = jnp.broadcast_to(
-        sectioned.reshape(blocks, 1, block_experts, MOST, width),
-        (blocks, PIECES, block_experts, MOST, width),
-    )
-    outgoing = outgoing.reshape(blocks * PIECES, block_experts, MOST, width)
-    gate_up = jnp.einsum(
-        "sgmd,gdf->sgmf",
-        lax.all_to_all(outgoing, "exp", split_axis=0, concat_axis=0, tiled=True),
-        gate_up_full,
-        preferred_element_type=jnp.float32,
-    )
-    activated = (jax.nn.silu(gate_up[..., :slice_width]) * gate_up[..., slice_width:]).astype(
-        jnp.bfloat16
-    )
-    computed = jnp.einsum(
-        "sgmf,gfd->sgmd", activated, down_full, preferred_element_type=jnp.float32
+    block_experts = w_gate_up.shape[1]
+    group = lax.axis_index("exp") // PIECES
+    named = expert_ids[:, :, None] == jnp.arange(ROUTE_LANES, dtype=jnp.int32)[None, None, :]
+    routing = jnp.sum(
+        jnp.where(named, expert_weights.astype(jnp.float32)[:, :, None], 0.0), axis=1
     ).astype(jnp.bfloat16)
-    returned = lax.all_to_all(computed, "exp", split_axis=0, concat_axis=0, tiled=True)
-    summed = jnp.sum(
-        returned.reshape(blocks, PIECES, block_experts, MOST, width), axis=1, dtype=jnp.float32
-    )
-    summed = summed.reshape(EXPERTS * MOST, width)
-    picked = summed[slot_index] * expert_weights.reshape(-1).astype(jnp.float32)[:, None]
-    mixture = jnp.sum(picked.reshape(rows_here, TOPK, width), axis=1)
-    layer_out = (attended.astype(jnp.float32) + residual_scale * mixture).astype(jnp.bfloat16)
+    gathered = lax.all_gather(
+        jnp.concatenate([moe_in, routing], axis=1), "exp", axis=0, tiled=True
+    )
+    partial = expert_sums(
+        group * block_experts, gathered, gate_up_full, down_full, width, block_experts
+    )
+    mixture = lax.psum_scatter(partial, "exp", scatter_dimension=0, tiled=True)
+    layer_out = (
+        attended.astype(jnp.float32) + residual_scale * mixture.astype(jnp.float32)
+    ).astype(jnp.bfloat16)
     return (attended, layer_out)
+
+
+def expert_kernel(first_ref, rows_ref, route_ref, gate_up_ref, down_ref, out_ref, total):
+    step = pl.program_id(1)
+    per_step = gate_up_ref.shape[1]
+    slice_width = down_ref.shape[2]
+    rows = rows_ref[...]
+    route = route_ref[...]
+    lane = lax.broadcasted_iota(jnp.int32, (ROUTE_LANES, slice_width), 0)
+    acts = []
+    for k in range(per_step):
+        weights = gate_up_ref[:, k].reshape(rows.shape[1], 2 * slice_width)
+        hidden = jnp.dot(rows, weights, preferred_element_type=jnp.float32)
+        gate, up = hidden[:, :slice_width], hidden[:, slice_width:]
+        pick = (lane == first_ref[0] + step * per_step + k).astype(jnp.bfloat16)
+        weight = jnp.dot(route, pick, preferred_element_type=jnp.float32)
+        acts.append((gate / (1.0 + jnp.exp(-gate)) * up * weight).astype(jnp.bfloat16))
+    act = jnp.concatenate(acts, axis=1)
+    parts = down_ref.shape[0]
+    columns = down_ref.shape[3]
+    for part in range(parts):
+        down = down_ref[part].reshape(per_step * slice_width, columns)
+        made = jnp.dot(act, down, preferred_element_type=jnp.float32)
+        where = slice(part * columns, (part + 1) * columns)
+
+        @pl.when(step == 0)
+        def _():
+            total[:, where] = made
+
+        @pl.when(step > 0)
+        def _():
+            total[:, where] += made
+
+    @pl.when(step == pl.num_programs(1) - 1)
+    def _():
+        out_ref[...] = total[...].astype(out_ref.dtype)
+
+
+def expert_sums(first, gathered, gate_up, down, width, block_experts):
+    count = gathered.shape[0]
+    tile = min(1024, count)
+    per_step = 2 if block_experts % 2 == 0 else 1
+    parts, _, depth, wide = gate_up.shape
+    _, _, slice_width, columns = down.shape
+    return pl.pallas_call(
+        expert_kernel,
+        grid_spec=pltpu.PrefetchScalarGridSpec(
+            num_scalar_prefetch=1,
+            grid=(count // tile, block_experts // per_step),
+            in_specs=[
+                pl.BlockSpec((tile, width), lambda i, s, first: (i, 0)),
+                pl.BlockSpec((tile, ROUTE_LANES), lambda i, s, first: (i, width // ROUTE_LANES)),
+                pl.BlockSpec((parts, per_step, depth, wide), lambda i, s, first: (0, s, 0, 0)),
+                pl.BlockSpec(
+                    (parts, per_step, slice_width, columns), lambda i, s, first: (0, s, 0, 0)
+                ),
+            ],
+            out_specs=pl.BlockSpec((tile, width), lambda i, s, first: (i, 0)),
+            scratch_shapes=[pltpu.VMEM((tile, width), jnp.float32)],
+        ),
+        out_shape=jax.ShapeDtypeStruct((count, width), jnp.bfloat16),
+        compiler_params=pltpu.CompilerParams(vmem_limit_bytes=50 * 1024 * 1024),
+        cost_estimate=pl.CostEstimate(
+            flops=6 * count * width * block_experts * slice_width,
+            bytes_accessed=6 * block_experts * width * slice_width + 4 * count * width,
+            transcendentals=count * block_experts * slice_width,
+        ),
+    )(jnp.full((1,), first, jnp.int32), gathered, gathered, gate_up, down)
 
 
 def solution(mesh):

time: 883 us -> 445 us (0.50)
  waiting for transfers between devices: 686 us -> 346 us
  local copies, waits for them, and re-layouts: 82.8 us -> 9.43 us
  Pallas kernels: 0 us -> 44.2 us
  matrix products: 46.8 us -> 17 us
  other arithmetic: 35.4 us -> 12.6 us
  starting transfers between devices: 11.7 us -> 0.2 us
    all_to_all x2 -> x0, waiting for transfers between devices: 578 us -> none  [the longest x1 333 us: shards(): lax.all_to_all(computed, 'exp', split_axis=0, concat_axis=0, tiled=True)]
    all_gather x2 -> x3, waiting for transfers between devices: 86.2 us -> 272 us  [the longest x1 150 us: shards(): lax.all_gather(w_gate_up[0], 'req', axis=0)]
    pallas_call x0 -> x1, Pallas kernels: none -> 44.2 us  [expert_sums(): pl.pallas_call(expert_kernel, grid_spec=pltpu.PrefetchScalarGridSpec(num_...]
    reduce_scatter x0 -> x1, waiting for transfers between devices: none -> 40.5 us  [shards(): mixture = lax.psum_scatter(partial, 'exp', scatter_dimension=0, tiled=True)]
    dot_general x2 -> x0, matrix products: 28.7 us -> none  [the longest x1 16.8 us: shards(): jnp.einsum('sgmd,gdf->sgmf', lax.all_to_all(outgoing, 'exp', split_axis=0...]
    scatter x1 -> x0, local copies, waits for them, and re-layouts: 18.1 us -> none  [shards(): jnp.zeros((EXPERTS * MOST, width), jnp.bfloat16).at[slot_index]]
    broadcast_in_dim x3 -> x0, local copies, waits for them, and re-layouts: 15.1 us -> none  [shards(): jnp.broadcast_to(sectioned.reshape(blocks, 1, block_experts, MOST, width)...]
    convert_element_type x2 -> x1, local copies, waits for them, and re-layouts: 14.1 us -> 0.11 us  [shards(): expert_weights.astype(jnp.float32)[:, :, None]]
  transfers between devices with their start and end apart: 5 -> 5, of which waited for: 4 -> 5; matrix products, arithmetic and copies ran while one was open for 10% -> 2% of each run, Pallas kernels for 0% -> 0%
where the time goes in v1:
time: 445 us; the launch traced here: 444 us
  waiting for transfers between devices  346 us (78%)
  Pallas kernels  44.2 us (10%)
  matrix products  17 us (4%)
  between operations  15 us (3%)
  other arithmetic  12.6 us (3%)
  local copies, waits for them, and re-layouts  9.43 us (2%)
    all_gather x1, waiting for transfers between devices, shards(): lax.all_gather(w_gate_up[0], 'req', axis=0)  150 us
    all_gather x1, waiting for transfers between devices, shards(): lax.all_gather(w_down[0], 'req', axis=0)  84 us
    pallas_call x1, Pallas kernels, expert_sums(): pl.pallas_call(expert_kernel, grid_spec=pltpu.PrefetchScalarGridSpec(num_...  44.2 us
    reduce_scatter x1, waiting for transfers between devices, shards(): mixture = lax.psum_scatter(partial, 'exp', scatter_dimension=0, tiled=True)  40.5 us
    all_gather x1, waiting for transfers between devices, shards(): lax.all_gather(jnp.concatenate([moe_in, routing], axis=1), 'exp', axis=0,...  38.1 us
    all_gather x1, waiting for transfers between devices, shards(): piece = lax.all_gather(joined, 'exp', axis=0, tiled=True)  31.5 us
  transfers between devices with their start and end apart: 5, of which 5 were waited for; matrix products, arithmetic and copies ran while one was open for 2% of the time, Pallas kernels for 0%

profile of v1, /device:TPU:0, one launch (start us, length us, event | category | flops | bytes accessed | tf_op | source)
XLA Modules:
  0.0 444.2 jit_solution(4562545699716748810)
XLA Ops:
  8.8 1.2 fusion.49
  10.1 1.8 fusion.83
  12.1 2.0 convolution_convert_fusion
  15.2 4.3 fusion.80
  22.3 31.5 %all-gather.5.cloned.1.call-done = bf16[1408,1024]{1,0:T(8,128)(2,1)} async-done(((bf16[176,1024]{1,0:T(8,128)(2,1)}), bf16[1408,1024]{1,0:T(8,128)(2,1)}) %all-gather.5.cloned.1.call-update) | async-done | bytes 2883600 | tf_op jit(solution)/shard_map/all_gather | solution.py:121
  53.8 1.7 fusion.89
  56.0 1.9 fusion.88
  57.9 1.9 copy.64
  59.8 1.0 copy.59
  61.3 1.1 fusion.1
  62.3 1.1 fusion
  64.3 1.5 fusion.2
  65.8 1.5 fusion.4
  67.3 1.1 fusion.7
  68.5 1.7 fusion.40
  70.3 1.7 fusion.34
  72.0 1.6 fusion.46
  76.9 38.1 %all-gather.7.cloned.1.call-done.rows_ref.route_ref = bf16[1024,1664]{1,0:T(8,128)(2,1)} async-done(((bf16[128,1664]{1,0:T(8,128)(2,1)}), bf16[1024,1664]{1,0:T(8,128)(2,1)}) %all-gather.7.cloned.1.call-update) | async-done | bytes 3407888 | tf_op jit(solution)/shard_map/all_gather | solution.py:159
  115.0 84.0 %all-gather.11.cloned.1.call-done.down_ref = bf16[4,20,128,384]{3,2,1,0:T(8,128)(2,1)} async-done(((bf16[1,20,128,384]{3,2,1,0:T(8,128)(2,1)}), bf16[4,20,128,384]{3,2,1,0:T(8,128)(2,1)}) %all-gather.11.cloned.1.call-update) | async-done | bytes 7864336 | tf_op jit(solution)/shard_map/all_gather | solution.py:96
  199.0 150.4 %all-gather.9.cloned.1.call-done.gate_up_ref = bf16[4,20,384,256]{3,2,1,0:T(8,128)(2,1)} async-done(((bf16[1,20,384,256]{3,2,1,0:T(8,128)(2,1)}), bf16[4,20,384,256]{3,2,1,0:T(8,128)(2,1)}) %all-gather.9.cloned.1.call-update) | async-done | bytes 15728656 | tf_op jit(solution)/shard_map/all_gather | solution.py:95
  349.4 44.2 %shard_map.140 = bf16[1024,1536]{1,0:T(8,128)(2,1)S(1)} custom-call(s32[1]{0:T(128)} %bitcast.37.first_ref, bf16[1024,1664]{1,0:T(8,128)(2,1)} %all-gather.7.cloned.1.call-done.rows_ref.route_ref, bf16[1024,1664]{1,0:T(8,128)(2,1)} %all-gather.7.cloned.1.call-done.rows_ref.route_ref, bf16[4,20,384,256]{3,2,1,0:T(8,128)(2,1)} %all-gather.9.cloned.1.call-done.gate_up_ref, ...), custom_call_target="tpu_custom_call" | custom-call | flops 24159191040 | bytes 29884416 | tf_op jit(solution)/shard_map/pallas_call | solution.py:214
  393.7 1.6 copy-done.2
  395.3 40.5 %reduce-scatter.2.cloned.1.call-done = bf16[128,1536]{1,0:T(8,128)(2,1)} async-done(((bf16[1024,1536]{1,0:T(8,128)(2,1)}), bf16[128,1536]{1,0:T(8,128)(2,1)}) %reduce-scatter.2.cloned.1.call-update) | async-done | bytes 393232 | tf_op jit(solution)/shard_map/reduce_scatter | solution.py:165
  435.8 1.8 fusion.55
  (73 shorter events, 10.0 us)
Async XLA Ops:
  7.2 2.9 copy-start
  7.2 8.0 %copy-start.3 = (bf16[128,1536]{1,0:T(8,128)(2,1)S(1)}, bf16[128,1536]{1,0:T(8,128)(2,1)}, u32[]{:S(2)}) copy-start(bf16[128,1536]{1,0:T(8,128)(2,1)} %param.13) | copy-start | bytes 1179652
  7.2 6.8 %copy-start.9 = (bf16[1,48,1024]{2,1,0:T(8,128)(2,1)S(1)}, bf16[1,48,1024]{2,1,0:T(8,128)(2,1)}, u32[]{:S(2)}) copy-start(bf16[1,48,1024]{2,1,0:T(8,128)(2,1)} %param.19) | copy-start | bytes 294916
  7.2 7.7 %copy-start.10 = (bf16[1536]{0:T(1024)(128)(2,1)S(1)}, bf16[1536]{0:T(1024)(128)(2,1)}, u32[]{:S(2)}) copy-start(bf16[1536]{0:T(1024)(128)(2,1)} %param.21) | copy-start | bytes 9220
  7.2 7.7 %copy-start.11 = (s32[128,8]{0,1:T(8,128)S(1)}, s32[128,8]{0,1:T(8,128)}, u32[]{:S(2)}) copy-start(s32[128,8]{0,1:T(8,128)} %param.22) | copy-start | bytes 12292
  7.2 7.8 %copy-start.12 = (bf16[128,8]{0,1:T(8,128)(2,1)S(1)}, bf16[128,8]{0,1:T(8,128)(2,1)}, u32[]{:S(2)}) copy-start(bf16[128,8]{0,1:T(8,128)(2,1)} %param.23) | copy-start | bytes 6148
  7.2 46.6 %all-gather.5.cloned.1.call-start = ((), (), s32[]{:S(2)}) async-start(), calls=%async_computation.1 | async-start | bytes 3244032 | tf_op jit(solution)/shard_map/all_gather | solution.py:121
  14.8 100.2 %all-gather.7.cloned.1.call-start = ((), (), s32[]{:S(2)}) async-start(), calls=%async_computation.2 | async-start | bytes 3833856 | tf_op jit(solution)/shard_map/all_gather | solution.py:159
  62.3 1.1 copy-start.5
  62.3 1.1 copy-start.7
  65.8 2.7 copy-start.6
  68.5 5.1 %slice-start = ((s8[4718592]{0:T(1024)(128)(4,1)}), s8[4194304]{0:T(1024)(128)(4,1)S(1)}, s32[]{:S(2)}) async-start(s8[4718592]{0:T(1024)(128)(4,1)} %bitcast.176), calls=%async_computation.6 | async-start | bytes 8388608
  70.3 3.3 slice-start.1
  73.6 1.1 copy-start.8
  74.5 361.3 %copy-start.4 = (bf16[128,1536]{1,0:T(8,128)(2,1)}, bf16[128,1536]{1,0:T(8,128)(2,1)S(1)}, u32[]{:S(2)}) copy-start(bf16[128,1536]{1,0:T(8,128)(2,1)S(1)} %get-tuple-element.30) | copy-start | bytes 1179652
  75.6 123.5 %all-gather.11.cloned.1.call-start = ((), (), s32[]{:S(2)}) async-start(), calls=%async_computation.4 | async-start | bytes 9830400 | tf_op jit(solution)/shard_map/all_gather | solution.py:96
  76.3 273.1 %all-gather.9.cloned.1.call-start = ((), (), s32[]{:S(2)}) async-start(), calls=%async_computation.3 | async-start | bytes 19660800 | tf_op jit(solution)/shard_map/all_gather | solution.py:95
  76.9 358.9 %reduce-scatter.2.cloned.1.call-start = ((), (), s32[]{:S(2)}) async-start(), calls=%async_computation.5 | async-start | bytes 3538944 | tf_op jit(solution)/shard_map/reduce_scatter | solution.py:165
  349.4 88.2 %copy-start.1 = (bf16[1536,512]{1,0:T(8,128)(2,1)S(1)}, bf16[1536,512]{1,0:T(8,128)(2,1)}, u32[]{:S(2)}) copy-start(bf16[1536,512]{1,0:T(8,128)(2,1)} %param.16) | copy-start | bytes 4718596
  393.6 1.6 copy-start.2
Sparse Core Ops, SparseCore 0:
  15.0 38.8 all-gather.4
  75.7 39.3 all-gather.6
  116.9 82.0 all-gather.10
  200.7 148.6 all-gather.8
  395.4 40.3 reduce-scatter.1

commit v2 on v1

--- a/solution.py
+++ b/solution.py
@@ -1,3 +1,5 @@
+import functools
+
 import jax
 import jax.numpy as jnp
 from jax import lax
@@ -8,6 +10,7 @@
 HEAD_DIM = 64
 PIECES = 4
 ROUTE_LANES = 128
+REQ_PARTS = 4
 
 
 rope_base = 10000.0
@@ -91,10 +94,9 @@
     length = cache_len[0]
     cache_rows = cache_kv[0]
     cache_count = cache_rows.shape[0]
-    gate_up_full, down_full = (
-        lax.all_gather(w_gate_up[0], "req", axis=0),
-        lax.all_gather(w_down[0], "req", axis=0),
-    )
+    half = (w_gate_up.shape[1] + 1) // 2
+    low, high = w_gate_up[0, :half], w_gate_up[0, half:]
+    low_1, low_2 = swap(low, 1), swap(low, 2)
     normed = rms_scale(hidden_in, attn_gain)
     query_pos = position_exp * rows_here + jnp.arange(rows_here, dtype=jnp.int32)
     positions = length + query_pos
@@ -119,6 +121,8 @@
     joined = jnp.concatenate([cache_rows, new_kv], axis=0)
     running = initial
     piece = lax.all_gather(joined, "exp", axis=0, tiled=True)
+    piece, low_1, low_2 = lax.optimization_barrier((piece, low_1, low_2))
+    high_1, high_2 = swap(high, 1), swap(high, 2)
     first_row = jnp.int32(0)
     key_count = piece.shape[0]
     for offset in range(0, key_count, key_block):
@@ -150,91 +154,122 @@
     projected = jnp.dot(context, w_out, preferred_element_type=jnp.float32)
     attended = (hidden_in.astype(jnp.float32) + residual_scale * projected).astype(jnp.bfloat16)
     moe_in = rms_scale(attended, moe_gain)
+    moe_in, high_1, high_2 = lax.optimization_barrier((moe_in, high_1, high_2))
+    low_3 = swap(low_2, 1)
+    high_3 = swap(high_1, 2)
     block_experts = w_gate_up.shape[1]
     group = lax.axis_index("exp") // PIECES
     named = expert_ids[:, :, None] == jnp.arange(ROUTE_LANES, dtype=jnp.int32)[None, None, :]
     routing = jnp.sum(
         jnp.where(named, expert_weights.astype(jnp.float32)[:, :, None], 0.0), axis=1
     ).astype(jnp.bfloat16)
+    part = width // REQ_PARTS
+    own = lax.axis_index("req")
+    sent = [
+        lax.dynamic_slice_in_dim(moe_in, (own ^ flip) * part, part, 1)
+        for flip in range(REQ_PARTS)
+    ]
     gathered = lax.all_gather(
-        jnp.concatenate([moe_in, routing], axis=1), "exp", axis=0, tiled=True
-    )
-    partial = expert_sums(
-        group * block_experts, gathered, gate_up_full, down_full, width, block_experts
-    )
-    mixture = lax.psum_scatter(partial, "exp", scatter_dimension=0, tiled=True)
+        jnp.concatenate(sent + [routing], axis=1), "exp", axis=0, tiled=True
+    )
+    first = group * block_experts
+    act_low = expert_acts(first, gathered, (low, low_1, low_2, low_3), width)
+    act_high = expert_acts(first + half, gathered, (high, high_1, high_2, high_3), width)
+    down, low_3, high_3 = lax.optimization_barrier((w_down[0], low_3, high_3))
+    down_1, down_2 = swap(down, 1), swap(down, 2)
+    down_3_low = swap(down_2[:half], 1)
+    down_3_high = swap(down_1[half:], 2)
+    act_high, down_3_low, down_3_high = lax.optimization_barrier(
+        (act_high, down_3_low, down_3_high)
+    )
+    made = [
+        jnp.dot(act_low, flat(rows[:half]), preferred_element_type=jnp.float32)
+        + jnp.dot(act_high, flat(rows[half:]), preferred_element_type=jnp.float32)
+        for rows in (down, down_1, down_2)
+    ]
+    made_3 = jnp.dot(act_low, flat(down_3_low), preferred_element_type=jnp.float32) + jnp.dot(
+        act_high, flat(down_3_high), preferred_element_type=jnp.float32
+    )
+    mixed = jnp.concatenate(
+        [
+            lax.psum_scatter(
+                jnp.concatenate(made, axis=1).astype(jnp.bfloat16),
+                "exp",
+                scatter_dimension=0,
+                tiled=True,
+            ),
+            lax.psum_scatter(
+                made_3.astype(jnp.bfloat16), "exp", scatter_dimension=0, tiled=True
+            ),
+        ],
+        axis=1,
+    )
+    mixture = jnp.concatenate(
+        [
+            lax.dynamic_slice_in_dim(mixed, (own ^ flip) * part, part, 1)
+            for flip in range(REQ_PARTS)
+        ],
+        axis=1,
+    )
     layer_out = (
         attended.astype(jnp.float32) + residual_scale * mixture.astype(jnp.float32)
     ).astype(jnp.bfloat16)
     return (attended, layer_out)
 
 
-def expert_kernel(first_ref, rows_ref, route_ref, gate_up_ref, down_ref, out_ref, total):
+def swap(values, flip):
+    return lax.ppermute(values, "req", [(r, r ^ flip) for r in range(REQ_PARTS)])
+
+
+def flat(rows):
+    return rows.reshape(rows.shape[0] * rows.shape[1], rows.shape[2])
+
+
+def act_kernel(per_step, first_ref, rows_ref, route_ref, *refs):
     step = pl.program_id(1)
-    per_step = gate_up_ref.shape[1]
-    slice_width = down_ref.shape[2]
+    gate_up_refs, out_ref = refs[:-1], refs[-1]
+    slice_width = gate_up_refs[0].shape[2] // 2
     rows = rows_ref[...]
     route = route_ref[...]
     lane = lax.broadcasted_iota(jnp.int32, (ROUTE_LANES, slice_width), 0)
-    acts = []
     for k in range(per_step):
-        weights = gate_up_ref[:, k].reshape(rows.shape[1], 2 * slice_width)
+        weights = jnp.concatenate([ref[k] for ref in gate_up_refs], axis=0)
         hidden = jnp.dot(rows, weights, preferred_element_type=jnp.float32)
         gate, up = hidden[:, :slice_width], hidden[:, slice_width:]
         pick = (lane == first_ref[0] + step * per_step + k).astype(jnp.bfloat16)
         weight = jnp.dot(route, pick, preferred_element_type=jnp.float32)
-        acts.append((gate / (1.0 + jnp.exp(-gate)) * up * weight).astype(jnp.bfloat16))
-    act = jnp.concatenate(acts, axis=1)
-    parts = down_ref.shape[0]
-    columns = down_ref.shape[3]
-    for part in range(parts):
-        down = down_ref[part].reshape(per_step * slice_width, columns)
-        made = jnp.dot(act, down, preferred_element_type=jnp.float32)
-        where = slice(part * columns, (part + 1) * columns)
-
-        @pl.when(step == 0)
-        def _():
-            total[:, where] = made
-
-        @pl.when(step > 0)
-        def _():
-            total[:, where] += made
-
-    @pl.when(step == pl.num_programs(1) - 1)
-    def _():
-        out_ref[...] = total[...].astype(out_ref.dtype)
-
-
-def expert_sums(first, gathered, gate_up, down, width, block_experts):
+        where = slice(k * slice_width, (k + 1) * slice_width)
+        out_ref[:, where] = (gate / (1.0 + jnp.exp(-gate)) * up * weight).astype(out_ref.dtype)
+
+
+def expert_acts(first, gathered, weights, width):
     count = gathered.shape[0]
     tile = min(1024, count)
-    per_step = 2 if block_experts % 2 == 0 else 1
-    parts, _, depth, wide = gate_up.shape
-    _, _, slice_width, columns = down.shape
+    experts, depth, wide = weights[0].shape
+    slice_width = wide // 2
+    per_step = 2 if experts % 2 == 0 else 1
+    in_specs = [
+        pl.BlockSpec((tile, width), lambda i, s, first: (i, 0)),
+        pl.BlockSpec((tile, ROUTE_LANES), lambda i, s, first: (i, width // ROUTE_LANES)),
+    ]
+    for _ in weights:
+        in_specs.append(pl.BlockSpec((per_step, depth, wide), lambda i, s, first: (s, 0, 0)))
     return pl.pallas_call(
-        expert_kernel,
+        functools.partial(act_kernel, per_step),
         grid_spec=pltpu.PrefetchScalarGridSpec(
             num_scalar_prefetch=1,
-            grid=(count // tile, block_experts // per_step),
-            in_specs=[
-                pl.BlockSpec((tile, width), lambda i, s, first: (i, 0)),
-                pl.BlockSpec((tile, ROUTE_LANES), lambda i, s, first: (i, width // ROUTE_LANES)),
-                pl.BlockSpec((parts, per_step, depth, wide), lambda i, s, first: (0, s, 0, 0)),
-                pl.BlockSpec(
-                    (parts, per_step, slice_width, columns), lambda i, s, first: (0, s, 0, 0)
-                ),
-            ],
-            out_specs=pl.BlockSpec((tile, width), lambda i, s, first: (i, 0)),
-            scratch_shapes=[pltpu.VMEM((tile, width), jnp.float32)],
+            grid=(count // tile, experts // per_step),
+            in_specs=in_specs,
+            out_specs=pl.BlockSpec((tile, per_step * slice_width), lambda i, s, first: (i, s)),
         ),
-        out_shape=jax.ShapeDtypeStruct((count, width), jnp.bfloat16),
-        compiler_params=pltpu.CompilerParams(vmem_limit_bytes=50 * 1024 * 1024),
+        out_shape=jax.ShapeDtypeStruct((count, experts * slice_width), jnp.bfloat16),
+        compiler_params=pltpu.CompilerParams(vmem_limit_bytes=40 * 1024 * 1024),
         cost_estimate=pl.CostEstimate(
-            flops=6 * count * width * block_experts * slice_width,
-            bytes_accessed=6 * block_experts * width * slice_width + 4 * count * width,
-            transcendentals=count * block_experts * slice_width,
+            flops=2 * count * width * experts * wide,
+            bytes_accessed=2 * (experts * width * wide + count * (width + experts * slice_width)),
+            transcendentals=count * experts * slice_width,
         ),
-    )(jnp.full((1,), first, jnp.int32), gathered, gathered, gate_up, down)
+    )(jnp.full((1,), first, jnp.int32), gathered, gathered, *weights)
 
 
 def solution(mesh):

time: 445 us -> 334 us (0.75)
  waiting for transfers between devices: 346 us -> 195 us
  local copies, waits for them, and re-layouts: 9.43 us -> 40.1 us
  Pallas kernels: 44.2 us -> 22.2 us
  matrix products: 17 us -> 37.3 us
  starting transfers between devices: 0.2 us -> 11.6 us
    all_gather x3 -> x1, waiting for transfers between devices: 272 us -> 0.01 us  [shards(): lax.all_gather(jnp.concatenate(sent + [routing], axis=1), 'exp', axis=0,...]
    ppermute x0 -> x10, waiting for transfers between devices: none -> 134 us  [swap(): lax.ppermute(values, 'req', [(r, r ^ flip) for r in range(REQ_PARTS)])]
    all_gather x1, waiting for transfers between devices: 31.5 us -> 0.01 us  [shards(): piece = lax.all_gather(joined, 'exp', axis=0, tiled=True)]
    pallas_call x1 -> x2, Pallas kernels: 44.2 us -> 22.2 us  [expert_acts(): pl.pallas_call(functools.partial(act_kernel, per_step), grid_spec=pltpu.P...]
    reduce_scatter x1 -> x2, waiting for transfers between devices: 40.5 us -> 61.4 us  [the longest x1 32 us: shards(): lax.psum_scatter(made_3.astype(jnp.bfloat16), 'exp', scatter_dimension=0,...]
    dot_general x0 -> x8, matrix products: none -> 19.1 us  [the longest x3 6.66 us: shards(): jnp.dot(act_low, flat(rows[:half]), preferred_element_type=jnp.float32)]
    ppermute x0 -> x10, starting transfers between devices: none -> 11.5 us  [swap(): lax.ppermute(values, 'req', [(r, r ^ flip) for r in range(REQ_PARTS)])]
    unnamed x31 -> x64, local copies, waits for them, and re-layouts: 1.81 us -> 11.7 us
  transfers between devices with their start and end apart: 5 -> 14, of which waited for: 5 -> 9; matrix products, arithmetic and copies ran while one was open for 2% -> 16% of each run, Pallas kernels for 0% -> 3%
where the time goes in v2:
time: 334 us; the launch traced here: 333 us
  waiting for transfers between devices  195 us (58%)
  local copies, waits for them, and re-layouts  40.1 us (12%)
  matrix products  37.3 us (11%)
  Pallas kernels  22.2 us (7%)
  between operations  15 us (4%)
  starting transfers between devices  11.6 us (3%)
  other arithmetic  11.4 us (3%)
    ppermute x10, waiting for transfers between devices, swap(): lax.ppermute(values, 'req', [(r, r ^ flip) for r in range(REQ_PARTS)])  134 us
    reduce_scatter x1, waiting for transfers between devices, shards(): lax.psum_scatter(made_3.astype(jnp.bfloat16), 'exp', scatter_dimension=0,...  32 us
    reduce_scatter x1, waiting for transfers between devices, shards(): lax.psum_scatter(jnp.concatenate(made, axis=1).astype(jnp.bfloat16), 'exp...  29.4 us
    pallas_call x2, Pallas kernels, expert_acts(): pl.pallas_call(functools.partial(act_kernel, per_step), grid_spec=pltpu.P...  22.2 us
    unnamed x64, local copies, waits for them, and re-layouts  11.7 us
    ppermute x10, starting transfers between devices, swap(): lax.ppermute(values, 'req', [(r, r ^ flip) for r in range(REQ_PARTS)])  11.5 us
    slice x5, local copies, waits for them, and re-layouts, attend_block(): block_rows[:, kv_width:].reshape(block_size, kv_heads, head_dim)  10.8 us
  transfers between devices with their start and end apart: 14, of which 9 were waited for; matrix products, arithmetic and copies ran while one was open for 16% of the time, Pallas kernels for 3%

profile of v2, /device:TPU:0, one launch (start us, length us, event | category | flops | bytes accessed | tf_op | source)
XLA Modules:
  0.0 333.1 jit_solution(248576289732811336)
XLA Ops:
  10.7 2.3 fusion.83
  14.9 3.8 %slice_bitcast_fusion = (bf16[10,384,256]{2,1,0:T(8,128)(2,1)}, bf16[10,384,256]{2,1,0:T(8,128)(2,1)S(1)}) fusion(bf16[1,20,384,256]{3,2,1,0:T(8,128)(2,1)} %param.24), kind=kLoop, calls=%fused_computation.24 | loop fusion | bytes 7864320 | tf_op jit(solution)/shard_map/squeeze | solution.py:98
  18.7 2.9 collective-permute-start
  24.0 4.7 %fusion.80 = f32[128,1536]{0,1:T(8,128)S(1)} fusion(bf16[1536,1536]{1,0:T(8,128)(2,1)} %param.15, bf16[128,1536]{1,0:T(8,128)(2,1)S(1)} %copy-done.12, f32[1536]{0:T(1024)S(1)} %convert_element_type.75, f32[128]{0:T(128)S(1)} %add_rsqrt_fusion.1), kind=kOutput, calls=%fused_computation.136 | convolution fusion | flops 604766208 | bytes 5904896 | tf_op jit(solution)/shard_map/dot_general | solution.py:104
  30.3 35.1 %collective-permute-done.refs_1_ = bf16[10,384,256]{2,1,0:T(8,128)(2,1)} collective-permute-done((bf16[10,384,256]{2,1,0:T(8,128)(2,1)S(1)}, bf16[10,384,256]{2,1,0:T(8,128)(2,1)}, u32[]{:S(2)}, u32[]{:S(2)}) %collective-permute-start) | collective-permute-done | bytes 1966112 | tf_op jit(solution)/shard_map/ppermute | solution.py:221
  65.4 2.1 collective-permute-done.1.refs_2_
  67.5 2.7 fusion.89
  72.2 2.1 copy.57
  78.5 2.1 copy.60
  82.5 2.1 fusion
  96.8 9.9 %collective-permute-done.2.refs_1_ = bf16[10,384,256]{2,1,0:T(8,128)(2,1)} collective-permute-done((bf16[10,384,256]{2,1,0:T(8,128)(2,1)}, bf16[10,384,256]{2,1,0:T(8,128)(2,1)}, u32[]{:S(2)}, u32[]{:S(2)}) %collective-permute-start.2) | collective-permute-done | bytes 1966112 | tf_op jit(solution)/shard_map/ppermute | solution.py:221
  113.6 41.5 %collective-permute-done.5.refs_3_ = bf16[10,384,256]{2,1,0:T(8,128)(2,1)S(1)} collective-permute-done((bf16[10,384,256]{2,1,0:T(8,128)(2,1)}, bf16[10,384,256]{2,1,0:T(8,128)(2,1)S(1)}, u32[]{:S(2)}, u32[]{:S(2)}) %collective-permute-start.5) | collective-permute-done | bytes 1966112 | tf_op jit(solution)/shard_map/ppermute | solution.py:221
  159.8 40.6 %collective-permute-done.6 = bf16[20,128,384]{2,1,0:T(8,128)(2,1)} collective-permute-done((bf16[20,128,384]{2,1,0:T(8,128)(2,1)}, bf16[20,128,384]{2,1,0:T(8,128)(2,1)}, u32[]{:S(2)}, u32[]{:S(2)}) %collective-permute-start.6) | collective-permute-done | bytes 1966112 | tf_op jit(solution)/shard_map/ppermute | solution.py:221
  200.4 3.1 fusion.92
  204.5 3.2 fusion.91
  213.9 11.2 %shard_map.141 = bf16[1024,1280]{1,0:T(8,128)(2,1)S(1)} custom-call(s32[1]{0:T(128)} %bitcast.42.first_ref, bf16[1024,1664]{1,0:T(8,128)(2,1)S(1)} %copy-done.2, bf16[1024,1664]{1,0:T(8,128)(2,1)S(1)} %copy-done.2, bf16[10,384,256]{2,1,0:T(8,128)(2,1)} %get-tuple-element.26.refs_0_, bf16[10,384,256]{2,1,0:T(8,128)(2,1)} %collective-permute-done.2.refs_1_, ...), custom_call_target="tpu_custom_call" | custom-call | flops 8053063680 | bytes 13631488 | tf_op jit(solution)/shard_map/pallas_call | solution.py:257
  225.2 3.2 collective-permute-done.9
  230.0 2.8 fusion.94
  235.4 11.0 %shard_map.140 = bf16[1024,1280]{1,0:T(8,128)(2,1)S(1)} custom-call(s32[1]{0:T(128)} %bitcast.38.first_ref, bf16[1024,1664]{1,0:T(8,128)(2,1)S(1)} %copy-done.3, bf16[1024,1664]{1,0:T(8,128)(2,1)S(1)} %copy-done.3, bf16[10,384,256]{2,1,0:T(8,128)(2,1)S(1)} %get-tuple-element.27.refs_0_, bf16[10,384,256]{2,1,0:T(8,128)(2,1)} %collective-permute-done.refs_1_, ...), custom_call_target="tpu_custom_call" | custom-call | flops 8053063680 | bytes 13631488 | tf_op jit(solution)/shard_map/pallas_call | solution.py:257
  246.4 3.6 %add_convert_fusion.1 = bf16[1024,384]{1,0:T(8,128)(2,1)S(1)} fusion(f32[1024,384]{1,0:T(8,128)S(1)} %fusion.95, bf16[1024,1280]{1,0:T(8,128)(2,1)S(1)} %shard_map.140, bf16[1280,384]{1,0:T(8,128)(2,1)} %bitcast.46), kind=kOutput, calls=%fused_computation.27 | convolution fusion | flops 1007419392 | bytes 5963776 | tf_op jit(solution)/shard_map/dot_general | solution.py:186
  255.7 2.9 fusion.96
  258.6 3.8 %add_convert_fusion = bf16[1024,384]{1,0:T(8,128)(2,1)} fusion(f32[1024,384]{1,0:T(8,128)S(1)} %fusion.96, bf16[1024,1280]{1,0:T(8,128)(2,1)S(1)} %copy-done.11, bf16[1280,384]{1,0:T(8,128)(2,1)} %bitcast.48), kind=kOutput, calls=%fused_computation.26 | convolution fusion | flops 1007419392 | bytes 5963776 | tf_op jit(solution)/shard_map/dot_general | solution.py:190
  262.4 29.4 %reduce-scatter.3.cloned.1.call-done = bf16[128,1152]{1,0:T(8,128)(2,1)} async-done(((bf16[1024,1152]{1,0:T(8,128)(2,1)}), bf16[128,1152]{1,0:T(8,128)(2,1)}) %reduce-scatter.3.cloned.1.call-update) | async-done | bytes 294928 | tf_op jit(solution)/shard_map/reduce_scatter | solution.py:195
  292.8 32.0 %reduce-scatter.5.cloned.1.call-done = bf16[128,384]{1,0:T(8,128)(2,1)} async-done(((bf16[1024,384]{1,0:T(8,128)(2,1)}), bf16[128,384]{1,0:T(8,128)(2,1)}) %reduce-scatter.5.cloned.1.call-update) | async-done | bytes 98320 | tf_op jit(solution)/shard_map/reduce_scatter | solution.py:201
  (139 shorter events, 60.0 us)
Async XLA Ops:
  7.2 6.8 %copy-start.23 = (bf16[1,48,1024]{2,1,0:T(8,128)(2,1)S(1)}, bf16[1,48,1024]{2,1,0:T(8,128)(2,1)}, u32[]{:S(2)}) copy-start(bf16[1,48,1024]{2,1,0:T(8,128)(2,1)} %param.19) | copy-start | bytes 294916
  7.2 60.3 %all-gather.3.cloned.1.call-start = ((), (), s32[]{:S(2)}) async-start(), calls=%async_computation.2 | async-start | bytes 3244032 | tf_op jit(solution)/shard_map/all_gather | solution.py:123
  14.8 8.9 %copy-start.24 = (bf16[1536]{0:T(1024)(128)(2,1)S(1)}, bf16[1536]{0:T(1024)(128)(2,1)}, u32[]{:S(2)}) copy-start(bf16[1536]{0:T(1024)(128)(2,1)} %param.21) | copy-start | bytes 9220
  14.8 8.9 %copy-start.26 = (bf16[128,8]{0,1:T(8,128)(2,1)S(1)}, bf16[128,8]{0,1:T(8,128)(2,1)}, u32[]{:S(2)}) copy-start(bf16[128,8]{0,1:T(8,128)(2,1)} %param.23) | copy-start | bytes 6148
  14.8 9.0 %copy-start.25 = (s32[128,8]{0,1:T(8,128)S(1)}, s32[128,8]{0,1:T(8,128)}, u32[]{:S(2)}) copy-start(s32[128,8]{0,1:T(8,128)} %param.22) | copy-start | bytes 12292
  14.8 9.2 %copy-start.12 = (bf16[128,1536]{1,0:T(8,128)(2,1)S(1)}, bf16[128,1536]{1,0:T(8,128)(2,1)}, u32[]{:S(2)}) copy-start(bf16[128,1536]{1,0:T(8,128)(2,1)} %param.13) | copy-start | bytes 1179652
  14.8 195.6 %all-gather.5.cloned.1.call-start = ((), (), s32[]{:S(2)}) async-start(), calls=%async_computation.3 | async-start | bytes 3833856 | tf_op jit(solution)/shard_map/all_gather | solution.py:172
  18.7 46.7 %collective-permute-start = (bf16[10,384,256]{2,1,0:T(8,128)(2,1)S(1)}, bf16[10,384,256]{2,1,0:T(8,128)(2,1)}, u32[]{:S(2)}, u32[]{:S(2)}) collective-permute-start(bf16[10,384,256]{2,1,0:T(8,128)(2,1)S(1)} %get-tuple-element.27.refs_0_), channel_id=1, source_target_pairs={{0,8},{8,0},{16,24},{24,16},{1,9},{9,1},{17,25},{25,17},{2,10},{10... | collective-permute-start | bytes 5898248 | tf_op jit(solution)/shard_map/ppermute | solution.py:221
  21.6 45.9 %collective-permute-start.1 = (bf16[10,384,256]{2,1,0:T(8,128)(2,1)S(1)}, bf16[10,384,256]{2,1,0:T(8,128)(2,1)}, u32[]{:S(2)}, u32[]{:S(2)}) collective-permute-start(bf16[10,384,256]{2,1,0:T(8,128)(2,1)S(1)} %get-tuple-element.27.refs_0_), channel_id=1, source_target_pairs={{0,16},{8,24},{16,0},{24,8},{1,17},{9,25},{17,1},{25,9},{2,18},{10... | collective-permute-start | bytes 5898248 | tf_op jit(solution)/shard_map/ppermute | solution.py:221
  23.2 83.5 %collective-permute-start.2 = (bf16[10,384,256]{2,1,0:T(8,128)(2,1)}, bf16[10,384,256]{2,1,0:T(8,128)(2,1)}, u32[]{:S(2)}, u32[]{:S(2)}) collective-permute-start(bf16[10,384,256]{2,1,0:T(8,128)(2,1)} %get-tuple-element.26.refs_0_), channel_id=1, source_target_pairs={{0,8},{8,0},{16,24},{24,16},{1,9},{9,1},{17,25},{25,17},{2,10},{10... | collective-permute-start | bytes 5898248 | tf_op jit(solution)/shard_map/ppermute | solution.py:221
  23.7 84.5 %collective-permute-start.3 = (bf16[10,384,256]{2,1,0:T(8,128)(2,1)}, bf16[10,384,256]{2,1,0:T(8,128)(2,1)}, u32[]{:S(2)}, u32[]{:S(2)}) collective-permute-start(bf16[10,384,256]{2,1,0:T(8,128)(2,1)} %get-tuple-element.26.refs_0_), channel_id=1, source_target_pairs={{0,16},{8,24},{16,0},{24,8},{1,17},{9,25},{17,1},{25,9},{2,18},{10... | collective-permute-start | bytes 5898248 | tf_op jit(solution)/shard_map/ppermute | solution.py:221
  96.6 229.1 %copy-start.13 = (bf16[128,1536]{1,0:T(8,128)(2,1)}, bf16[128,1536]{1,0:T(8,128)(2,1)S(1)}, u32[]{:S(2)}) copy-start(bf16[128,1536]{1,0:T(8,128)(2,1)S(1)} %get-tuple-element.62) | copy-start | bytes 1179652
  111.4 180.4 %reduce-scatter.3.cloned.1.call-start = ((), (), s32[]{:S(2)}) async-start(), calls=%async_computation.4 | async-start | bytes 2654208 | tf_op jit(solution)/shard_map/reduce_scatter | solution.py:195
  111.4 43.6 %collective-permute-start.5 = (bf16[10,384,256]{2,1,0:T(8,128)(2,1)}, bf16[10,384,256]{2,1,0:T(8,128)(2,1)S(1)}, u32[]{:S(2)}, u32[]{:S(2)}) collective-permute-start(bf16[10,384,256]{2,1,0:T(8,128)(2,1)} %collective-permute-done.2.refs_1_), channel_id=1, source_target_pairs={{0,16},{8,24},{16,0},{24,8},{1,17},{9,25},{17,1},{25,9},{2,18},{10... | collective-permute-start | bytes 5898248 | tf_op jit(solution)/shard_map/ppermute | solution.py:221
  113.0 43.3 %collective-permute-start.4 = (bf16[10,384,256]{2,1,0:T(8,128)(2,1)}, bf16[10,384,256]{2,1,0:T(8,128)(2,1)S(1)}, u32[]{:S(2)}, u32[]{:S(2)}) collective-permute-start(bf16[10,384,256]{2,1,0:T(8,128)(2,1)} %collective-permute-done.1.refs_2_), channel_id=1, source_target_pairs={{0,8},{8,0},{16,24},{24,16},{1,9},{9,1},{17,25},{25,17},{2,10},{10... | collective-permute-start | bytes 5898248 | tf_op jit(solution)/shard_map/ppermute | solution.py:221
  157.6 42.8 %collective-permute-start.6 = (bf16[20,128,384]{2,1,0:T(8,128)(2,1)}, bf16[20,128,384]{2,1,0:T(8,128)(2,1)}, u32[]{:S(2)}, u32[]{:S(2)}) collective-permute-start(bf16[20,128,384]{2,1,0:T(8,128)(2,1)} %bitcast.211), channel_id=1, source_target_pairs={{0,16},{8,24},{16,0},{24,8},{1,17},{9,25},{17,1},{25,9},{2,18},{10... | collective-permute-start | bytes 5898248 | tf_op jit(solution)/shard_map/ppermute | solution.py:221
  159.2 45.3 %collective-permute-start.8 = (bf16[20,128,384]{2,1,0:T(8,128)(2,1)}, bf16[20,128,384]{2,1,0:T(8,128)(2,1)}, u32[]{:S(2)}, u32[]{:S(2)}) collective-permute-start(bf16[20,128,384]{2,1,0:T(8,128)(2,1)} %bitcast.212), channel_id=1, source_target_pairs={{0,8},{8,0},{16,24},{24,16},{1,9},{9,1},{17,25},{25,17},{2,10},{10... | collective-permute-start | bytes 5898248 | tf_op jit(solution)/shard_map/ppermute | solution.py:221
  159.8 49.1 %copy-start.14 = (bf16[1,20,128,384]{3,2,1,0:T(8,128)(2,1)S(1)}, bf16[1,20,128,384]{3,2,1,0:T(8,128)(2,1)}, u32[]{:S(2)}) copy-start(bf16[1,20,128,384]{3,2,1,0:T(8,128)(2,1)} %param.25) | copy-start | bytes 5898244
  203.5 21.7 %collective-permute-start.7 = (bf16[10,128,384]{2,1,0:T(8,128)(2,1)}, bf16[10,128,384]{2,1,0:T(8,128)(2,1)}, u32[]{:S(2)}, u32[]{:S(2)}) collective-permute-start(bf16[10,128,384]{2,1,0:T(8,128)(2,1)} %get-tuple-element.39), channel_id=1, source_target_pairs={{0,8},{8,0},{16,24},{24,16},{1,9},{9,1},{17,25},{25,17},{2,10},{10... | collective-permute-start | bytes 2949128 | tf_op jit(solution)/shard_map/ppermute | solution.py:221
  207.6 20.8 %collective-permute-start.9 = (bf16[10,128,384]{2,1,0:T(8,128)(2,1)}, bf16[10,128,384]{2,1,0:T(8,128)(2,1)}, u32[]{:S(2)}, u32[]{:S(2)}) collective-permute-start(bf16[10,128,384]{2,1,0:T(8,128)(2,1)} %get-tuple-element.37), channel_id=1, source_target_pairs={{0,16},{8,24},{16,0},{24,8},{1,17},{9,25},{17,1},{25,9},{2,18},{10... | collective-permute-start | bytes 2949128 | tf_op jit(solution)/shard_map/ppermute | solution.py:221
  213.9 14.5 %copy-start.18 = (bf16[10,128,384]{2,1,0:T(8,128)(2,1)S(1)}, bf16[10,128,384]{2,1,0:T(8,128)(2,1)}, u32[]{:S(2)}) copy-start(bf16[10,128,384]{2,1,0:T(8,128)(2,1)} %get-tuple-element.38) | copy-start | bytes 2949124
  225.2 7.6 %copy-start.8 = (bf16[1024,1280]{1,0:T(8,128)(2,1)}, bf16[1024,1280]{1,0:T(8,128)(2,1)S(1)}, u32[]{:S(2)}) copy-start(bf16[1024,1280]{1,0:T(8,128)(2,1)S(1)} %shard_map.141) | copy-start | bytes 7864324
  254.8 69.9 %reduce-scatter.5.cloned.1.call-start = ((), (), s32[]{:S(2)}) async-start(), calls=%async_computation.5 | async-start | bytes 884736 | tf_op jit(solution)/shard_map/reduce_scatter | solution.py:201
  258.6 68.0 %copy-start.1 = (bf16[1536,512]{1,0:T(8,128)(2,1)S(1)}, bf16[1536,512]{1,0:T(8,128)(2,1)}, u32[]{:S(2)}) copy-start(bf16[1536,512]{1,0:T(8,128)(2,1)} %param.17) | copy-start | bytes 4718596
  (19 other events, 46.5 us)
Sparse Core Ops, SparseCore 0:
  14.9 38.8 all-gather.2
  111.5 40.7 all-gather.4
  254.9 36.7 reduce-scatter.2
  293.9 30.7 reduce-scatter.4

commit v3 on v2

--- a/solution.py
+++ b/solution.py
@@ -177,32 +177,24 @@
     act_high = expert_acts(first + half, gathered, (high, high_1, high_2, high_3), width)
     down, low_3, high_3 = lax.optimization_barrier((w_down[0], low_3, high_3))
     down_1, down_2 = swap(down, 1), swap(down, 2)
+    act = jnp.concatenate([act_low, act_high], axis=1)
+    act, act_low, act_high, down_1, down_2 = lax.optimization_barrier(
+        (act, act_low, act_high, down_1, down_2)
+    )
     down_3_low = swap(down_2[:half], 1)
     down_3_high = swap(down_1[half:], 2)
-    act_high, down_3_low, down_3_high = lax.optimization_barrier(
-        (act_high, down_3_low, down_3_high)
-    )
     made = [
-        jnp.dot(act_low, flat(rows[:half]), preferred_element_type=jnp.float32)
-        + jnp.dot(act_high, flat(rows[half:]), preferred_element_type=jnp.float32)
+        jnp.dot(act, flat(rows), preferred_element_type=jnp.float32).astype(jnp.bfloat16)
         for rows in (down, down_1, down_2)
     ]
     made_3 = jnp.dot(act_low, flat(down_3_low), preferred_element_type=jnp.float32) + jnp.dot(
         act_high, flat(down_3_high), preferred_element_type=jnp.float32
     )
-    mixed = jnp.concatenate(
-        [
-            lax.psum_scatter(
-                jnp.concatenate(made, axis=1).astype(jnp.bfloat16),
-                "exp",
-                scatter_dimension=0,
-                tiled=True,
-            ),
-            lax.psum_scatter(
-                made_3.astype(jnp.bfloat16), "exp", scatter_dimension=0, tiled=True
-            ),
-        ],
-        axis=1,
+    mixed = lax.psum_scatter(
+        jnp.concatenate(made + [made_3.astype(jnp.bfloat16)], axis=1),
+        "exp",
+        scatter_dimension=0,
+        tiled=True,
     )
     mixture = jnp.concatenate(
         [

time: 334 us -> 274 us (0.82)
  waiting for transfers between devices: 195 us -> 152 us
  local copies, waits for them, and re-layouts: 40.1 us -> 25.8 us
  matrix products: 37.3 us -> 33.1 us
    ppermute x10, waiting for transfers between devices: 134 us -> 112 us  [swap(): lax.ppermute(values, 'req', [(r, r ^ flip) for r in range(REQ_PARTS)])]
    reduce_scatter x2 -> x1, waiting for transfers between devices: 61.4 us -> 40 us  [shards(): lax.psum_scatter(jnp.concatenate(made + [made_3.astype(jnp.bfloat16)], ax...]
    unnamed x64 -> x41, local copies, waits for them, and re-layouts: 11.7 us -> 3.04 us
    slice x3 -> x2, local copies, waits for them, and re-layouts: 7.79 us -> 2.6 us  [the longest x1 1.3 us: shards(): down_3_high = swap(down_1[half:], 2)]
    dot_general x6 -> x3, matrix products: 12.5 us -> 11.7 us  [shards(): jnp.dot(act, flat(rows), preferred_element_type=jnp.float32)]
  transfers between devices with their start and end apart: 14 -> 13, of which waited for: 9 -> 11; matrix products, arithmetic and copies ran while one was open for 16% -> 20% of each run, Pallas kernels for 3% -> 8%
where the time goes in v3:
time: 274 us; the launch traced here: 273 us
  waiting for transfers between devices  152 us (55%)
  matrix products  33.1 us (12%)
  local copies, waits for them, and re-layouts  25.8 us (9%)
  Pallas kernels  22.6 us (8%)
  between operations  15 us (5%)
  starting transfers between devices  12.5 us (5%)
  other arithmetic  11.8 us (4%)
    ppermute x10, waiting for transfers between devices, swap(): lax.ppermute(values, 'req', [(r, r ^ flip) for r in range(REQ_PARTS)])  112 us
    reduce_scatter x1, waiting for transfers between devices, shards(): lax.psum_scatter(jnp.concatenate(made + [made_3.astype(jnp.bfloat16)], ax...  40 us
    pallas_call x2, Pallas kernels, expert_acts(): pl.pallas_call(functools.partial(act_kernel, per_step), grid_spec=pltpu.P...  22.6 us
    ppermute x10, starting transfers between devices, swap(): lax.ppermute(values, 'req', [(r, r ^ flip) for r in range(REQ_PARTS)])  12.4 us
    dot_general x3, matrix products, shards(): jnp.dot(act, flat(rows), preferred_element_type=jnp.float32)  11.7 us
    slice x5, local copies, waits for them, and re-layouts, attend_block(): block_rows[:, kv_width:].reshape(block_size, kv_heads, head_dim)  10.8 us
  transfers between devices with their start and end apart: 13, of which 11 were waited for; matrix products, arithmetic and copies ran while one was open for 20% of the time, Pallas kernels for 8%

profile of v3, /device:TPU:0, one launch (start us, length us, event | category | flops | bytes accessed | tf_op | source)
XLA Modules:
  0.0 272.9 jit_solution(10069068256500679141)
XLA Ops:
  12.0 2.0 convolution_convert_fusion.3
  14.9 3.9 %slice_bitcast_fusion = (bf16[10,384,256]{2,1,0:T(8,128)(2,1)S(1)}, bf16[10,384,256]{2,1,0:T(8,128)(2,1)}) fusion(bf16[1,20,384,256]{3,2,1,0:T(8,128)(2,1)} %param.24), kind=kLoop, calls=%fused_computation.25 | loop fusion | bytes 7864320 | tf_op jit(solution)/shard_map/squeeze | solution.py:98
  18.7 3.0 %collective-permute-start = (bf16[10,384,256]{2,1,0:T(8,128)(2,1)}, bf16[10,384,256]{2,1,0:T(8,128)(2,1)}, u32[]{:S(2)}, u32[]{:S(2)}) collective-permute-start(bf16[10,384,256]{2,1,0:T(8,128)(2,1)} %get-tuple-element.31.refs_0_), channel_id=1, source_target_pairs={{0,8},{8,0},{16,24},{24,16},{1,9},{9,1},{17,25},{25,17},{2,10},{10... | collective-permute-start | bytes 5898248 | tf_op jit(solution)/shard_map/ppermute | solution.py:213
  24.1 4.7 %fusion.80 = f32[128,1536]{0,1:T(8,128)S(1)} fusion(bf16[1536,1536]{1,0:T(8,128)(2,1)} %param.15, bf16[128,1536]{1,0:T(8,128)(2,1)S(1)} %copy-done.4, f32[1536]{0:T(1024)S(1)} %convert_element_type.83, f32[128]{0:T(128)S(1)} %add_rsqrt_fusion.1), kind=kOutput, calls=%fused_computation.135 | convolution fusion | flops 604766208 | bytes 5904896 | tf_op jit(solution)/shard_map/dot_general | solution.py:104
  30.3 35.3 %collective-permute-done.refs_1_ = bf16[10,384,256]{2,1,0:T(8,128)(2,1)} collective-permute-done((bf16[10,384,256]{2,1,0:T(8,128)(2,1)}, bf16[10,384,256]{2,1,0:T(8,128)(2,1)}, u32[]{:S(2)}, u32[]{:S(2)}) %collective-permute-start) | collective-permute-done | bytes 1966112 | tf_op jit(solution)/shard_map/ppermute | solution.py:213
  65.7 2.1 collective-permute-done.1.refs_2_
  67.8 2.7 fusion.89
  70.5 2.0 fusion.88
  74.8 2.0 copy.60
  76.7 2.1 copy.55
  78.8 2.0 copy.58
  80.9 1.9 copy.61
  82.8 2.1 fusion.1
  97.3 9.7 %collective-permute-done.2.refs_1_ = bf16[10,384,256]{2,1,0:T(8,128)(2,1)} collective-permute-done((bf16[10,384,256]{2,1,0:T(8,128)(2,1)S(1)}, bf16[10,384,256]{2,1,0:T(8,128)(2,1)}, u32[]{:S(2)}, u32[]{:S(2)}) %collective-permute-start.2) | collective-permute-done | bytes 1966112 | tf_op jit(solution)/shard_map/ppermute | solution.py:213
  111.5 41.6 %collective-permute-done.4.refs_3_ = bf16[10,384,256]{2,1,0:T(8,128)(2,1)} collective-permute-done((bf16[10,384,256]{2,1,0:T(8,128)(2,1)}, bf16[10,384,256]{2,1,0:T(8,128)(2,1)}, u32[]{:S(2)}, u32[]{:S(2)}) %collective-permute-start.4) | collective-permute-done | bytes 1966112 | tf_op jit(solution)/shard_map/ppermute | solution.py:213
  156.5 2.0 copy-done.2
  158.4 11.4 %shard_map.140 = bf16[1024,1280]{1,0:T(8,128)(2,1)S(1)} custom-call(s32[1]{0:T(128)} %bitcast.38.first_ref, bf16[1024,1664]{1,0:T(8,128)(2,1)S(1)} %copy-done.2, bf16[1024,1664]{1,0:T(8,128)(2,1)S(1)} %copy-done.2, bf16[10,384,256]{2,1,0:T(8,128)(2,1)} %get-tuple-element.31.refs_0_, bf16[10,384,256]{2,1,0:T(8,128)(2,1)} %collective-permute-done.refs_1_, ...), custom_call_target="tpu_custom_call" | custom-call | flops 8053063680 | bytes 13631488 | tf_op jit(solution)/shard_map/pallas_call | solution.py:249
  169.8 11.2 %shard_map.141 = bf16[1024,1280]{1,0:T(8,128)(2,1)S(1)} custom-call(s32[1]{0:T(128)} %bitcast.40.first_ref, bf16[1024,1664]{1,0:T(8,128)(2,1)S(1)} %copy-done.3, bf16[1024,1664]{1,0:T(8,128)(2,1)S(1)} %copy-done.3, bf16[10,384,256]{2,1,0:T(8,128)(2,1)S(1)} %get-tuple-element.30.refs_0_, bf16[10,384,256]{2,1,0:T(8,128)(2,1)} %collective-permute-done.2.refs_1_, ...), custom_call_target="tpu_custom_call" | custom-call | flops 8053063680 | bytes 13631488 | tf_op jit(solution)/shard_map/pallas_call | solution.py:249
  181.4 14.9 %collective-permute-done.6 = bf16[20,128,384]{2,1,0:T(8,128)(2,1)} collective-permute-done((bf16[20,128,384]{2,1,0:T(8,128)(2,1)}, bf16[20,128,384]{2,1,0:T(8,128)(2,1)}, u32[]{:S(2)}, u32[]{:S(2)}) %collective-permute-start.6) | collective-permute-done | bytes 1966112 | tf_op jit(solution)/shard_map/ppermute | solution.py:213
  202.1 2.9 %convolution_convert_fusion.2 = bf16[1024,384]{1,0:T(8,128)(2,1)S(1)} fusion(bf16[1024,2560]{1,0:T(8,128)(2,1)S(1)} %pad_maximum_fusion, bf16[2560,384]{1,0:T(8,128)(2,1)S(1)} %bitcast.212), kind=kOutput, calls=%fused_computation.30 | convolution fusion | flops 2013659136 | bytes 7995392 | tf_op jit(solution)/shard_map/dot_general | solution.py:187
  204.9 4.4 %convolution_convert_fusion.1 = bf16[1024,384]{1,0:T(8,128)(2,1)S(1)} fusion(bf16[1024,2560]{1,0:T(8,128)(2,1)S(1)} %pad_maximum_fusion, bf16[2560,384]{1,0:T(8,128)(2,1)} %bitcast.43), kind=kOutput, calls=%fused_computation.29 | convolution fusion | flops 2013659136 | bytes 7995392 | tf_op jit(solution)/shard_map/dot_general | solution.py:187
  209.3 4.4 %convolution_convert_fusion = bf16[1024,384]{1,0:T(8,128)(2,1)S(1)} fusion(bf16[1024,2560]{1,0:T(8,128)(2,1)S(1)} %pad_maximum_fusion, bf16[2560,384]{1,0:T(8,128)(2,1)} %bitcast.44), kind=kOutput, calls=%fused_computation.28 | convolution fusion | flops 2013659136 | bytes 7995392 | tf_op jit(solution)/shard_map/dot_general | solution.py:187
  213.8 4.5 %collective-permute-done.9 = bf16[10,128,384]{2,1,0:T(8,128)(2,1)S(1)} collective-permute-done((bf16[10,128,384]{2,1,0:T(8,128)(2,1)S(1)}, bf16[10,128,384]{2,1,0:T(8,128)(2,1)S(1)}, u32[]{:S(2)}, u32[]{:S(2)}) %collective-permute-start.9) | collective-permute-done | bytes 983072 | tf_op jit(solution)/shard_map/ppermute | solution.py:213
  224.4 40.0 %reduce-scatter.2.cloned.1.call-done = bf16[128,1536]{1,0:T(8,128)(2,1)} async-done(((bf16[1024,1536]{1,0:T(8,128)(2,1)}), bf16[128,1536]{1,0:T(8,128)(2,1)}) %reduce-scatter.2.cloned.1.call-update) | async-done | bytes 393232 | tf_op jit(solution)/shard_map/reduce_scatter | solution.py:193
  (109 shorter events, 45.2 us)
Async XLA Ops:
  7.2 6.8 %copy-start.11 = (bf16[1,48,1024]{2,1,0:T(8,128)(2,1)S(1)}, bf16[1,48,1024]{2,1,0:T(8,128)(2,1)}, u32[]{:S(2)}) copy-start(bf16[1,48,1024]{2,1,0:T(8,128)(2,1)} %param.19) | copy-start | bytes 294916
  7.2 60.6 %all-gather.3.cloned.1.call-start = ((), (), s32[]{:S(2)}) async-start(), calls=%async_computation.1 | async-start | bytes 3244032 | tf_op jit(solution)/shard_map/all_gather | solution.py:123
  14.0 9.8 %copy-start.12 = (bf16[1536]{0:T(1024)(128)(2,1)S(1)}, bf16[1536]{0:T(1024)(128)(2,1)}, u32[]{:S(2)}) copy-start(bf16[1536]{0:T(1024)(128)(2,1)} %param.21) | copy-start | bytes 9220
  14.0 9.8 %copy-start.13 = (s32[128,8]{0,1:T(8,128)S(1)}, s32[128,8]{0,1:T(8,128)}, u32[]{:S(2)}) copy-start(s32[128,8]{0,1:T(8,128)} %param.22) | copy-start | bytes 12292
  14.0 9.9 %copy-start.14 = (bf16[128,8]{0,1:T(8,128)(2,1)S(1)}, bf16[128,8]{0,1:T(8,128)(2,1)}, u32[]{:S(2)}) copy-start(bf16[128,8]{0,1:T(8,128)(2,1)} %param.23) | copy-start | bytes 6148
  14.0 10.1 %copy-start.4 = (bf16[128,1536]{1,0:T(8,128)(2,1)S(1)}, bf16[128,1536]{1,0:T(8,128)(2,1)}, u32[]{:S(2)}) copy-start(bf16[128,1536]{1,0:T(8,128)(2,1)} %param.13) | copy-start | bytes 1179652
  14.8 141.6 %all-gather.5.cloned.1.call-start = ((), (), s32[]{:S(2)}) async-start(), calls=%async_computation.2 | async-start | bytes 3833856 | tf_op jit(solution)/shard_map/all_gather | solution.py:172
  18.7 46.9 %collective-permute-start = (bf16[10,384,256]{2,1,0:T(8,128)(2,1)}, bf16[10,384,256]{2,1,0:T(8,128)(2,1)}, u32[]{:S(2)}, u32[]{:S(2)}) collective-permute-start(bf16[10,384,256]{2,1,0:T(8,128)(2,1)} %get-tuple-element.31.refs_0_), channel_id=1, source_target_pairs={{0,8},{8,0},{16,24},{24,16},{1,9},{9,1},{17,25},{25,17},{2,10},{10... | collective-permute-start | bytes 5898248 | tf_op jit(solution)/shard_map/ppermute | solution.py:213
  21.7 46.1 %collective-permute-start.1 = (bf16[10,384,256]{2,1,0:T(8,128)(2,1)}, bf16[10,384,256]{2,1,0:T(8,128)(2,1)}, u32[]{:S(2)}, u32[]{:S(2)}) collective-permute-start(bf16[10,384,256]{2,1,0:T(8,128)(2,1)} %get-tuple-element.31.refs_0_), channel_id=1, source_target_pairs={{0,16},{8,24},{16,0},{24,8},{1,17},{9,25},{17,1},{25,9},{2,18},{10... | collective-permute-start | bytes 5898248 | tf_op jit(solution)/shard_map/ppermute | solution.py:213
  23.2 83.7 %collective-permute-start.2 = (bf16[10,384,256]{2,1,0:T(8,128)(2,1)S(1)}, bf16[10,384,256]{2,1,0:T(8,128)(2,1)}, u32[]{:S(2)}, u32[]{:S(2)}) collective-permute-start(bf16[10,384,256]{2,1,0:T(8,128)(2,1)S(1)} %get-tuple-element.30.refs_0_), channel_id=1, source_target_pairs={{0,8},{8,0},{16,24},{24,16},{1,9},{9,1},{17,25},{25,17},{2,10},{10... | collective-permute-start | bytes 5898248 | tf_op jit(solution)/shard_map/ppermute | solution.py:213
  23.7 84.7 %collective-permute-start.3 = (bf16[10,384,256]{2,1,0:T(8,128)(2,1)S(1)}, bf16[10,384,256]{2,1,0:T(8,128)(2,1)}, u32[]{:S(2)}, u32[]{:S(2)}) collective-permute-start(bf16[10,384,256]{2,1,0:T(8,128)(2,1)S(1)} %get-tuple-element.30.refs_0_), channel_id=1, source_target_pairs={{0,16},{8,24},{16,0},{24,8},{1,17},{9,25},{17,1},{25,9},{2,18},{10... | collective-permute-start | bytes 5898248 | tf_op jit(solution)/shard_map/ppermute | solution.py:213
  91.1 5.1 %slice-start = ((s8[4718592]{0:T(1024)(128)(4,1)}), s8[4194304]{0:T(1024)(128)(4,1)S(1)}, s32[]{:S(2)}) async-start(s8[4718592]{0:T(1024)(128)(4,1)} %bitcast.197), calls=%async_computation.4 | async-start | bytes 8388608
  92.8 3.3 %slice-start.1 = ((s8[4718592]{0:T(1024)(128)(4,1)}), s8[524288]{0:T(1024)(128)(4,1)S(1)}, s32[]{:S(2)}) async-start(s8[4718592]{0:T(1024)(128)(4,1)} %bitcast.197), calls=%async_computation.5 | async-start | bytes 1048576
  97.1 168.4 %copy-start.5 = (bf16[128,1536]{1,0:T(8,128)(2,1)}, bf16[128,1536]{1,0:T(8,128)(2,1)S(1)}, u32[]{:S(2)}) copy-start(bf16[128,1536]{1,0:T(8,128)(2,1)S(1)} %get-tuple-element.60) | copy-start | bytes 1179652
  109.4 155.0 %reduce-scatter.2.cloned.1.call-start = ((), (), s32[]{:S(2)}) async-start(), calls=%async_computation.3 | async-start | bytes 3538944 | tf_op jit(solution)/shard_map/reduce_scatter | solution.py:193
  109.4 43.7 %collective-permute-start.4 = (bf16[10,384,256]{2,1,0:T(8,128)(2,1)}, bf16[10,384,256]{2,1,0:T(8,128)(2,1)}, u32[]{:S(2)}, u32[]{:S(2)}) collective-permute-start(bf16[10,384,256]{2,1,0:T(8,128)(2,1)} %collective-permute-done.1.refs_2_), channel_id=1, source_target_pairs={{0,8},{8,0},{16,24},{24,16},{1,9},{9,1},{17,25},{25,17},{2,10},{10... | collective-permute-start | bytes 5898248 | tf_op jit(solution)/shard_map/ppermute | solution.py:213
  109.8 43.7 %collective-permute-start.5 = (bf16[10,384,256]{2,1,0:T(8,128)(2,1)}, bf16[10,384,256]{2,1,0:T(8,128)(2,1)}, u32[]{:S(2)}, u32[]{:S(2)}) collective-permute-start(bf16[10,384,256]{2,1,0:T(8,128)(2,1)} %collective-permute-done.2.refs_1_), channel_id=1, source_target_pairs={{0,16},{8,24},{16,0},{24,8},{1,17},{9,25},{17,1},{25,9},{2,18},{10... | collective-permute-start | bytes 5898248 | tf_op jit(solution)/shard_map/ppermute | solution.py:213
  153.6 42.8 %collective-permute-start.6 = (bf16[20,128,384]{2,1,0:T(8,128)(2,1)}, bf16[20,128,384]{2,1,0:T(8,128)(2,1)}, u32[]{:S(2)}, u32[]{:S(2)}) collective-permute-start(bf16[20,128,384]{2,1,0:T(8,128)(2,1)} %bitcast.210), channel_id=1, source_target_pairs={{0,8},{8,0},{16,24},{24,16},{1,9},{9,1},{17,25},{25,17},{2,10},{10... | collective-permute-start | bytes 5898248 | tf_op jit(solution)/shard_map/ppermute | solution.py:213
  154.9 42.2 %collective-permute-start.7 = (bf16[20,128,384]{2,1,0:T(8,128)(2,1)}, bf16[20,128,384]{2,1,0:T(8,128)(2,1)}, u32[]{:S(2)}, u32[]{:S(2)}) collective-permute-start(bf16[20,128,384]{2,1,0:T(8,128)(2,1)} %bitcast.211), channel_id=1, source_target_pairs={{0,16},{8,24},{16,0},{24,8},{1,17},{9,25},{17,1},{25,9},{2,18},{10... | collective-permute-start | bytes 5898248 | tf_op jit(solution)/shard_map/ppermute | solution.py:213
  158.4 11.4 %copy-start.3 = (bf16[1024,1664]{1,0:T(8,128)(2,1)S(1)}, bf16[1024,1664]{1,0:T(8,128)(2,1)}, u32[]{:S(2)}) copy-start(bf16[1024,1664]{1,0:T(8,128)(2,1)} %all-gather.5.cloned.1.call-done.rows_ref.route_ref) | copy-start | bytes 10223620
  181.0 21.1 %copy-start.15 = (bf16[1,20,128,384]{3,2,1,0:T(8,128)(2,1)S(1)}, bf16[1,20,128,384]{3,2,1,0:T(8,128)(2,1)}, u32[]{:S(2)}) copy-start(bf16[1,20,128,384]{3,2,1,0:T(8,128)(2,1)} %param.25) | copy-start | bytes 5898244
  198.4 19.9 %collective-permute-start.9 = (bf16[10,128,384]{2,1,0:T(8,128)(2,1)S(1)}, bf16[10,128,384]{2,1,0:T(8,128)(2,1)S(1)}, u32[]{:S(2)}, u32[]{:S(2)}) collective-permute-start(bf16[10,128,384]{2,1,0:T(8,128)(2,1)S(1)} %slice.64), channel_id=1, source_target_pairs={{0,16},{8,24},{16,0},{24,8},{1,17},{9,25},{17,1},{25,9},{2,18},{10... | collective-permute-start | bytes 2949128 | tf_op jit(solution)/shard_map/ppermute | solution.py:213
  201.3 19.7 %collective-permute-start.8 = (bf16[10,128,384]{2,1,0:T(8,128)(2,1)S(1)}, bf16[10,128,384]{2,1,0:T(8,128)(2,1)S(1)}, u32[]{:S(2)}, u32[]{:S(2)}) collective-permute-start(bf16[10,128,384]{2,1,0:T(8,128)(2,1)S(1)} %slice.63), channel_id=1, source_target_pairs={{0,8},{8,0},{16,24},{24,16},{1,9},{9,1},{17,25},{25,17},{2,10},{10... | collective-permute-start | bytes 2949128 | tf_op jit(solution)/shard_map/ppermute | solution.py:213
  221.0 45.3 %copy-start.1 = (bf16[1536,512]{1,0:T(8,128)(2,1)S(1)}, bf16[1536,512]{1,0:T(8,128)(2,1)}, u32[]{:S(2)}) copy-start(bf16[1536,512]{1,0:T(8,128)(2,1)} %param.16) | copy-start | bytes 4718596
  (7 other events, 12.9 us)
Sparse Core Ops, SparseCore 0:
  14.9 38.8 all-gather.2
  109.5 40.7 all-gather.4
  224.5 39.8 reduce-scatter.1
